TPU v7x, 512 devices: a whole 4x4x16 slice. The times are simulated.
512 devices in a mesh: replica: 4 (over z_lo), fsdp: 16 (over y, x), tensor: 8 (over z_hi, core).
Axes of the slice: x: 4, y: 4, z: 16 (z_hi: 4, z_lo: 4; z = z_hi * 4 + z_lo), core: 2. Of those that a mesh axis runs over, the one named last changes fastest.
Arguments:
- inputs: bfloat16 [32768, 8192], P(('replica', 'fsdp'), 'tensor'), may hold values from -0.032958984 to 0.032958984
- kv_grad: bfloat16 [32768, 2048], P(('replica', 'fsdp'), 'tensor'), may hold values from -6 to 6
- weight_blocks: bfloat16 [8, 128, 128, 128], P('tensor', 'fsdp'), may hold values from -0.1875 to 0.1875
- bitmap: int32 [64, 16], P('tensor'), may hold values from 0 to 1, as said below
- counts: int32 [8, 16], P('tensor'), may hold values from 0 to 8, as said below
Outputs:
- input_grad: bfloat16 [32768, 8192], P(('replica', 'fsdp'), 'tensor')
- weight_grad: float32 [8, 128, 128, 128], P('tensor', 'fsdp')
Inputs may be any that keep to these rules, and one draw needn't show every extreme that they name: `bitmap`: in every band of 8 rows (rows b * 8 to (b + 1) * 8 - 1) exactly 64 entries are 1. `counts`: each row sums to 64 and its largest entry is 8.
All inputs are finite; a program needn't handle non-finite values.
Results may differ from a plain program's by a relative error of at most 0.001.
Values may be sent and summed in bfloat16 or wider, within the bound.
A program may use at most 64 MiB of HBM per device.

v0:
```python
import jax
import jax.numpy as jnp
from jax import lax
from jax.sharding import PartitionSpec as P


def block_places(bit_flags, packed):
    ranking = jnp.cumsum(bit_flags) - 1
    matches = (bit_flags[None, :] == 1) & (ranking[None, :] == packed[:, None])
    places = jnp.arange(bit_flags.shape[0], dtype=jnp.int32)
    return jnp.sum(jnp.where(matches, places[None, :], 0), axis=1)


def body(inputs, kv_grad, weight_blocks, bitmap, counts):
    block_side = weight_blocks.shape[-1]
    flat_size = block_side * block_side
    tokens_here = inputs.shape[0]
    rows_here = inputs.shape[1] // block_side
    capacity = weight_blocks.shape[1]
    shard_total = lax.axis_size("fsdp")
    col_width = bitmap.shape[1]
    positions = rows_here * col_width
    live_total = positions // 2
    per_shard = live_total // shard_total
    bit_flags = bitmap.reshape(-1)
    shard_counts = counts[0]
    offsets = jnp.cumsum(shard_counts) - shard_counts
    shard_ids = jnp.arange(shard_total, dtype=jnp.int32)
    slot_ids = jnp.arange(shard_total * capacity, dtype=jnp.int32)
    source = slot_ids // capacity
    slot_local = slot_ids - source * capacity
    source_match = source[:, None] == shard_ids[None, :]
    slot_packed = jnp.sum(jnp.where(source_match, offsets[None, :], 0), axis=1) + slot_local
    slot_valid = slot_local < jnp.sum(jnp.where(source_match, shard_counts[None, :], 0), axis=1)
    slot_places = block_places(bit_flags, slot_packed)
    place_ids = jnp.arange(positions, dtype=jnp.int32)
    placing = (slot_places[None, :] == place_ids[:, None]) & slot_valid[None, :]
    full_grads = lax.all_gather(kv_grad, "tensor", axis=1, tiled=True)
    grad_blocks = full_grads.reshape(tokens_here, col_width, block_side)
    row_blocks = inputs.reshape(tokens_here, rows_here, block_side)
    owned_blocks = weight_blocks[0]
    part_blocks = lax.all_gather(owned_blocks, "fsdp", axis=0, tiled=True)
    part_count = part_blocks.shape[0]
    columns = placing.astype(jnp.bfloat16)
    dense_blocks = jnp.dot(
        columns, part_blocks.reshape(part_count, flat_size), preferred_element_type=jnp.float32
    )
    dense_blocks = dense_blocks.astype(jnp.bfloat16).reshape(
        rows_here, col_width, block_side, block_side
    )
    input_grad = jnp.einsum(
        "tjh,ijdh->tid", grad_blocks, dense_blocks, preferred_element_type=jnp.float32
    )
    input_grad = input_grad.reshape(tokens_here, rows_here * block_side).astype(jnp.bfloat16)
    outer_terms = jnp.einsum(
        "tid,tjh->ijdh", row_blocks, grad_blocks, preferred_element_type=jnp.float32
    )
    outer_terms = outer_terms.reshape(positions, flat_size)
    numbers = jnp.arange(live_total, dtype=jnp.int32)
    live_places = block_places(bit_flags, numbers)
    picking = (live_places[:, None] == place_ids[None, :]).astype(jnp.float32)
    selected = jnp.dot(
        picking, outer_terms, precision=lax.Precision.HIGHEST, preferred_element_type=jnp.float32
    )
    shares = lax.psum_scatter(
        selected.reshape(per_shard * lax.axis_size("fsdp"), block_side, block_side),
        "fsdp",
        scatter_dimension=0,
        tiled=True,
    )
    summed = lax.all_gather(shares, "fsdp", axis=0, tiled=True).reshape(live_total, flat_size)
    itself = shard_ids == lax.axis_index("fsdp")
    own_offset = jnp.sum(jnp.where(itself, offsets, 0))
    own_count = jnp.sum(jnp.where(itself, shard_counts, 0))
    own_slots = jnp.arange(capacity, dtype=jnp.int32)
    wanted = own_offset + own_slots
    choose = ((wanted[:, None] == numbers[None, :]) & (own_slots < own_count)[:, None]).astype(
        jnp.float32
    )
    result = jnp.dot(
        choose, summed, precision=lax.Precision.HIGHEST, preferred_element_type=jnp.float32
    )
    result = result.reshape(capacity, block_side, block_side)
    result = lax.psum(result, "replica")
    return (input_grad, result[None])


def solution(mesh):
    in_specs = (
        P(("replica", "fsdp"), "tensor"),
        P(("replica", "fsdp"), "tensor"),
        P("tensor", "fsdp", None, None),
        P("tensor", None),
        P("tensor", None),
    )
    out_specs = (P(("replica", "fsdp"), "tensor"), P("tensor", "fsdp", None, None))
    return jax.shard_map(body, mesh=mesh, in_specs=in_specs, out_specs=out_specs, check_vma=False)
```

profile of v0, /device:TPU:2, one launch (start us, length us, event | category | flops | bytes accessed | tf_op | source)
XLA Modules:
  0.0 434.2 jit_solution(9738321089910467430)
XLA Ops:
  7.2 0.0 copy-start
  7.2 0.0 all-gather.5.cloned.1.call-start
  7.2 1.9 copy.39
  9.1 0.0 all-gather.5.cloned.1.call-update
  9.1 0.0 reduce-scatter.2.cloned.1.call-start
  9.2 0.8 reshape.145
  9.9 0.7 broadcast_compare_fusion
  10.6 0.1 eq.101
  10.7 0.2 reduce-window.13
  10.9 0.1 add_reduce_fusion
  11.0 0.1 select_reduce_fusion.1
  11.1 65.7 %all-gather.5.cloned.1.call-done = bf16[512,2048]{0,1:T(8,128)(2,1)} async-done(((bf16[512,256]{0,1:T(8,128)(2,1)}), bf16[512,2048]{0,1:T(8,128)(2,1)}) %all-gather.5.cloned.1.call-update) | async-done | bytes 2097168 | tf_op jit(solution)/shard_map/all_gather | solution.py:38
  76.8 0.0 copy-done
  76.8 7.1 %convolution_bitcast_fusion = f32[8,16,128,128]{2,3,0,1:T(8,128)} fusion(bf16[512,16,128,1]{0,2,3,1:T(8,128)(2,1)} %bitcast.98, bf16[512,1024]{1,0:T(8,128)(2,1)S(1)} %copy-done), kind=kOutput, calls=%fused_computation.10 | convolution fusion | flops 2147483648 | bytes 11534336 | tf_op jit(solution)/shard_map/tid,tjh->ijdh/dot_general | solution.py:55
  84.0 9.1 %copy.42 = f32[8,16,128,128]{3,2,1,0:T(8,128)} copy(f32[8,16,128,128]{2,3,0,1:T(8,128)} %convolution_bitcast_fusion) | data formatting | bytes 16777216 | tf_op jit(solution)/shard_map/tid,tjh->ijdh/transpose | solution.py:55
  93.1 13.1 %copy.79 = f32[16,8,128,128]{3,1,2,0:T(8,128)} copy(f32[16,8,128,128]{3,2,1,0:T(8,128)} %bitcast.89) | data formatting | bytes 16777216
  106.2 9.0 %copy.52 = f32[16384,128]{1,0:T(8,128)} copy(f32[16384,128]{0,1:T(8,128)} %bitcast.90) | data formatting | bytes 16777216 | tf_op jit(solution)/shard_map/dot_general | solution.py:62
  115.2 7.6 %fusion.21 = f32[64,128,128]{2,0,1:T(8,128)S(1)} fusion(f32[128,128,128]{2,1,0:T(8,128)} %bitcast.88, s32[64]{0:T(128)S(1)} %select_reduce_fusion.1), kind=kOutput, calls=%fused_computation.26 | convolution fusion | flops 1610620928 | bytes 12583168 | tf_op jit(solution)/shard_map/dot_general | solution.py:62
  122.8 4.4 %copy.44 = f32[64,128,128]{2,1,0:T(8,128)} copy(f32[64,128,128]{2,0,1:T(8,128)S(1)} %fusion.21) | data formatting | bytes 8388608 | tf_op jit(solution)/shard_map/dot_general | solution.py:62
  127.2 0.0 copy-start.1
  127.2 0.0 reduce-scatter.2.cloned.1.call-update
  127.3 0.0 all-gather.9.cloned.1.call-start
  127.3 0.7 all-gather.9.cloned.1.call-update
  128.0 0.0 all-gather.7.cloned.1.call-start
  128.1 88.4 %reduce-scatter.2.cloned.1.call-done = f32[4,128,128]{2,1,0:T(8,128)} async-done(((f32[64,128,128]{2,1,0:T(8,128)}), f32[4,128,128]{2,1,0:T(8,128)}) %reduce-scatter.2.cloned.1.call-update) | async-done | bytes 262160 | tf_op jit(solution)/shard_map/reduce_scatter | solution.py:65
  216.5 0.0 all-gather.7.cloned.1.call-update
  216.5 0.0 all-reduce.2.cloned.1.call-start
  216.6 0.0 copy-done.1
  216.6 0.1 copy.37
  216.7 0.1 reduce.1
  216.8 0.6 fusion.31
  217.4 0.6 iota_compare_fusion.5
  218.1 0.7 iota_add_fusion
  218.8 0.1 select_reduce_fusion.2
  218.9 0.2 select_reduce_fusion
  219.1 67.5 %all-gather.9.cloned.1.call-done = bf16[1,128,128,128]{3,2,0,1:T(8,128)(2,1)} async-done(((bf16[1,8,128,128]{3,2,0,1:T(8,128)(2,1)}), bf16[1,128,128,128]{3,2,0,1:T(8,128)(2,1)}) %all-gather.9.cloned.1.call-update) | async-done | bytes 4194320 | tf_op jit(solution)/shard_map/all_gather | solution.py:42
  286.6 5.4 %fusion.7 = bf16[16,8,128,128]{3,1,2,0:T(8,128)(2,1)S(1)} fusion(bf16[16,8,128,128]{3,2,1,0:T(8,128)(2,1)} %bitcast.92, s32[128]{0:T(128)S(1)} %select_reduce_fusion, pred[128]{0:T(512)(128)(4,1)S(1)} %fusion.33), kind=kOutput, calls=%fused_computation.11 | convolution fusion | flops 539000832 | bytes 8389248 | tf_op jit(solution)/shard_map/dot_general | solution.py:45
  292.0 3.2 copy.56
  295.2 61.4 %all-gather.7.cloned.1.call-done = f32[64,128,128]{2,1,0:T(8,128)} async-done(((f32[4,128,128]{2,1,0:T(8,128)}), f32[64,128,128]{2,1,0:T(8,128)}) %all-gather.7.cloned.1.call-update) | async-done | bytes 4194320 | tf_op jit(solution)/shard_map/all_gather | solution.py:71
  356.6 6.6 %fusion.12 = f32[1,8,128,128]{3,1,2,0:T(8,128)} fusion(s32[8]{0:T(128)S(1)} %iota_add_fusion, pred[8]{0:T(512)(128)(4,1)S(1)} %iota_compare_fusion.5, f32[8,8,128,128]{3,2,1,0:T(8,128)} %bitcast.91), kind=kOutput, calls=%fused_computation.13 | convolution fusion | flops 100664320 | bytes 4718632 | tf_op jit(solution)/shard_map/dot_general | solution.py:80
  363.1 0.0 all-reduce.2.cloned.1.call-update
  363.1 5.2 %bitcast_convert_fusion = bf16[8,128,512]{2,1,0:T(8,128)(2,1)S(1)} fusion(bf16[512,16,128,1]{0,2,1,3:T(8,128)(2,1)} %bitcast.99, bf16[8,16,128,128]{3,2,1,0:T(8,128)(2,1)} %bitcast.93), kind=kOutput, calls=%fused_computation.12 | convolution fusion | flops 2148007936 | bytes 7340032 | tf_op jit(solution)/shard_map/tjh,ijdh->tid/dot_general | solution.py:51
  368.3 1.3 copy.46
  369.7 56.1 %all-reduce.2.cloned.1.call-done = f32[1,8,128,128]{3,1,2,0:T(8,128)} async-done(((f32[1,8,128,128]{3,1,2,0:T(8,128)}), f32[1,8,128,128]{3,1,2,0:T(8,128)}) %all-reduce.2.cloned.1.call-update) | async-done | bytes 524304 | tf_op jit(solution)/shard_map/psum | solution.py:84
  425.7 1.9 copy.47
  (5 shorter events, 0.1 us)
Async XLA Ops:
  7.2 69.6 %copy-start = (bf16[512,1024]{1,0:T(8,128)(2,1)S(1)}, bf16[512,1024]{1,0:T(8,128)(2,1)}, u32[]{:S(2)}) copy-start(bf16[512,1024]{1,0:T(8,128)(2,1)} %param.5) | copy-start | bytes 3145732
  7.2 69.6 %all-gather.5.cloned.1.call-start = ((), (), s32[]{:S(2)}) async-start(), calls=%async_computation.1 | async-start | bytes 2359296 | tf_op jit(solution)/shard_map/all_gather | solution.py:38
  9.1 207.4 %reduce-scatter.2.cloned.1.call-start = ((), (), s32[]{:S(2)}) async-start(), calls=%async_computation.2 | async-start | bytes 4456448 | tf_op jit(solution)/shard_map/reduce_scatter | solution.py:65
  127.2 89.3 %copy-start.1 = (s32[1,16]{1,0:T(1,128)S(1)}, s32[1,16]{1,0:T(1,128)}, u32[]{:S(2)}) copy-start(s32[1,16]{1,0:T(1,128)} %param.9) | copy-start | bytes 196
  127.3 159.3 %all-gather.9.cloned.1.call-start = ((), (), s32[]{:S(2)}) async-start(), calls=%async_computation.5 | async-start | bytes 4456448 | tf_op jit(solution)/shard_map/all_gather | solution.py:42
  128.0 228.5 %all-gather.7.cloned.1.call-start = ((), (), s32[]{:S(2)}) async-start(), calls=%async_computation.3 | async-start | bytes 4456448 | tf_op jit(solution)/shard_map/all_gather | solution.py:71
  216.5 209.2 %all-reduce.2.cloned.1.call-start = ((), (), s32[]{:S(2)}) async-start(), calls=%async_computation.4 | async-start | bytes 1048576 | tf_op jit(solution)/shard_map/psum | solution.py:84
Sparse Core Ops, SparseCore 0:
  10.7 66.0 all-gather.4
  127.4 89.0 reduce-scatter.1
  219.9 66.6 all-gather.8
  289.9 66.6 all-gather.6
  363.3 62.4 all-reduce.1
where the time goes:
time: 435 us; the launch traced here: 434 us
  waiting for transfers between devices  340 us (78%)
  local copies, waits for them, and re-layouts  44.9 us (10%)
  matrix products  31.9 us (7%)
  between operations  13.9 us (3%)
    reduce_scatter x1, waiting for transfers between devices, body(): lax.psum_scatter(selected.reshape(per_shard * lax.axis_size('fsdp'), bloc...  88.4 us
    all_gather x1, waiting for transfers between devices, body(): part_blocks = lax.all_gather(owned_blocks, 'fsdp', axis=0, tiled=True)  67.5 us
    all_gather x1, waiting for transfers between devices, body(): full_grads = lax.all_gather(kv_grad, 'tensor', axis=1, tiled=True)  65.7 us
    all_gather x1, waiting for transfers between devices, body(): lax.all_gather(shares, 'fsdp', axis=0, tiled=True)  61.4 us
    psum x1, waiting for transfers between devices, body(): result = lax.psum(result, 'replica')  56.1 us
    unnamed x9, local copies, waits for them, and re-layouts  21.4 us
    dot_general x2, local copies, waits for them, and re-layouts, body(): jnp.dot(picking, outer_terms, precision=lax.Precision.HIGHEST, preferred_...  13.4 us
    transpose x1, local copies, waits for them, and re-layouts, body(): jnp.einsum('tid,tjh->ijdh', row_blocks, grad_blocks, preferred_element_ty...  9.13 us
  transfers between devices with their start and end apart: 5, of which 5 were waited for; matrix products, arithmetic and copies ran while one was open for 4% of the time, Pallas kernels for 0%

commit v1 on v0

v1 whole, which is shorter than its diff:
```python
import functools

import jax
import jax.numpy as jnp
from jax import lax
from jax.experimental import pallas as pl
from jax.experimental.pallas import tpu as pltpu
from jax.sharding import PartitionSpec as P

MESH = pl.DeviceIdType.MESH
RADIUS = 32700.0
STEPS = 16.0
LIFT = 2048.0
PIECES = 4
M_R, M_L, O_R, O_L, C_R, C_L = range(6)


def encode(buf, count, k, block):
    half = block.shape[0] // 2
    peak = jnp.maximum(jnp.max(jnp.abs(block), axis=0, keepdims=True), 1e-30)
    code = (jnp.log(peak) * STEPS + LIFT).astype(jnp.int32) + 1
    scale = jnp.exp((code.astype(jnp.float32) - LIFT) * (1.0 / STEPS))
    whole = jnp.round(block * (RADIUS / scale)).astype(jnp.int32)
    buf[pl.ds(pl.multiple_of(k * half, half), half), :] = whole[:half] * 65536 + whole[half:]
    buf[pl.ds(count * half + k, 1), :] = code


def decode(buf, count, k, side):
    half = side // 2
    pair = buf[pl.ds(pl.multiple_of(k * half, half), half), :]
    code = buf[pl.ds(count * half + k, 1), :]
    scale = jnp.exp((code.astype(jnp.float32) - LIFT) * (1.0 / STEPS)) * (1.0 / RADIUS)
    low = (pair << 16) >> 16
    high = (pair - low) >> 16
    return jnp.concatenate([high.astype(jnp.float32), low.astype(jnp.float32)], axis=0) * scale


def kernel(
    slot_place, place_slot, shard_counts, inputs, kv_grad, weights,
    input_grad, weight_grad,
    x_in, x_turned, kvg, wg, dense, terms, grad_out, part, total,
    send1, recv1, send2, recv2, zsend1, zrecv1, zsend2, zrecv2,
    local_sem, kv_send, kv_recv, w_send, w_recv, rs_send, rs_recv, z_send, z_recv,
):
    rep = lax.axis_index("replica")
    shard = lax.axis_index("fsdp")
    band = lax.axis_index("tensor")
    tokens, width = x_in.shape
    side = terms.shape[-1]
    cap = weights.shape[1]
    cols = kv_grad.shape[1]
    hc = cap // 2
    ring = 4
    rows, groups = width // side, 8
    col_blocks = cols // side * groups
    piece = tokens // PIECES

    def shift(f, axis, by):
        y, x = f // ring, f % ring
        if axis == "x":
            return y * ring + (x + by + ring) % ring
        return ((y + by + ring) % ring) * ring + x

    def near(axis, by):
        return {"fsdp": shift(shard, axis, by)}

    def band_at(by):
        return (band + 2 * by + groups) % groups

    sibling = band + 1 - 2 * (band % 2)

    def sibling_at(by):
        return (sibling + 2 * by + groups) % groups

    def remote(src, dst, send_sem, recv_sem, where):
        return pltpu.make_async_remote_copy(
            src_ref=src, dst_ref=dst, send_sem=send_sem, recv_sem=recv_sem,
            device_id=where, device_id_type=MESH,
        )

    partners = [{"tensor": sibling}, {"tensor": band_at(1)}, {"tensor": band_at(-1)}]
    partners += [near(axis, by) for axis in ("x", "y") for by in (1, -1)]
    partners += [{"replica": (rep + d) % 4} for d in (1, 2, 3)]
    barrier = pltpu.get_barrier_semaphore()
    for where in partners:
        pl.semaphore_signal(barrier, inc=1, device_id=where, device_id_type=MESH)
    pl.semaphore_wait(barrier, len(partners))

    sent = []

    def go(copy):
        copy.start()
        sent.append(copy)

    def kv_at(b, p, n=1):
        return kvg.at[b, pl.ds(p * piece, n * piece), :]

    own_kv = [kv_grad.at[pl.ds(p * piece, piece), :] for p in range(PIECES)]
    right_order = list(range(PIECES))
    left_order = right_order[PIECES // 2:] + right_order[:PIECES // 2]
    for a, b in zip(right_order, left_order):
        go(remote(own_kv[a], kv_at(band, a), kv_send.at[0, a], kv_recv.at[0, a], {"tensor": band_at(1)}))
        go(remote(own_kv[b], kv_at(band, b), kv_send.at[1, b], kv_recv.at[1, b], {"tensor": band_at(-1)}))

    firsts = ("x", "y")
    seconds = ("y", "x")

    def w_at(f, slot, n):
        return wg.at[pl.ds(f * cap + slot, n)]

    for h in range(2):
        own_w = weights.at[0, pl.ds(hc * h, hc)]
        for d, by in ((0, 1), (1, -1)):
            go(remote(own_w, w_at(shard, hc * h, hc), w_send.at[h, 0, d], w_recv.at[h, 0, d], near(firsts[h], by)))
            go(remote(own_w, w_at(shard, hc * h, hc), w_send.at[h, 2, d], w_recv.at[h, 2, d], near(seconds[h], by)))
    go(remote(kv_grad, kv_at(band, 0, PIECES), kv_send.at[3, 0], kv_recv.at[3, 0], {"tensor": sibling}))
    local = [
        pltpu.make_async_copy(inputs, x_in, local_sem.at[0]),
        pltpu.make_async_copy(kv_grad, kvg.at[band], local_sem.at[1]),
        pltpu.make_async_copy(weights.at[0], w_at(shard, 0, cap), local_sem.at[2]),
    ]
    for copy in local:
        copy.start()

    def kv_wait(which, p, b, n=1):
        remote(kv_at(b, p, n), kv_at(b, p, n), kv_send.at[which, p], kv_recv.at[which, p], {"tensor": sibling}).wait_recv()

    def kv_pass(which, p, b):
        go(remote(kv_at(b, p), kv_at(b, p), kv_send.at[which, p], kv_recv.at[which, p], {"tensor": sibling}))

    def kv_relay(p, b, by):
        go(remote(kv_at(b, p), kv_at(b, p), kv_send.at[2, p], kv_recv.at[2, p], {"tensor": band_at(by)}))

    def w_wait(h, which, d, f, slot, n):
        at = w_at(f, hc * h + slot, n)
        remote(at, at, w_send.at[h, which, d], w_recv.at[h, which, d], {"tensor": sibling}).wait_recv()

    def w_go(h, which, d, f, slot, n, axis):
        at = w_at(f, hc * h + slot, n)
        go(remote(at, at, w_send.at[h, which, d], w_recv.at[h, which, d], near(axis, 1 if d == 0 else -1)))

    hq = hc // 2

    def w_first(h):
        for d, by in ((0, -1), (1, 1)):
            src = shift(shard, firsts[h], by)
            w_wait(h, 0, d, src, 0, hc)
            w_go(h, 1, d, src, d * hq, hq, firsts[h])
            for e in range(2):
                w_go(h, 3 + d, e, src, 0, hc, seconds[h])

    def w_far(h):
        src = shift(shard, firsts[h], 2)
        for d in range(2):
            w_wait(h, 1, d, src, d * hq, hq)
        for e in range(2):
            w_go(h, 5, e, src, 0, hc, seconds[h])

    def w_second(h, s):
        for d, by in ((0, -1), (1, 1)):
            src = shift(shift(shard, firsts[h], (0, -1, 1, 2)[s]), seconds[h], by)
            w_wait(h, 2 + s, d, src, 0, hc)
            w_go(h, 6 + s, d, src, d * hq, hq, seconds[h])

    def w_last(h, s):
        src = shift(shift(shard, firsts[h], (0, -1, 1, 2)[s]), seconds[h], 2)
        for d in range(2):
            w_wait(h, 6 + s, d, src, d * hq, hq)

    def outer(b):
        def tile(i, carry):
            at = pl.ds(pl.multiple_of(i * 2 * side, 2 * side), 2 * side)
            got = jnp.dot(x_turned[at, :], kvg[b], preferred_element_type=jnp.float32)
            for u in range(2):
                for v in range(2):
                    place = (2 * i + u) * col_blocks + 2 * b + v
                    terms[place] = got[u * side:(u + 1) * side, v * side:(v + 1) * side]
            return carry

        lax.fori_loop(0, rows // 2, tile, 0)

    local[0].wait()
    local[1].wait()
    x_turned[...] = x_in[...].T
    for h in range(2):
        w_first(h)
    outer(band)
    for p, q in ((0, 2), (1, 3)):
        kv_wait(0, p, band_at(-1))
        kv_relay(p, band_at(-1), 1)
        kv_wait(1, q, band_at(1))
        kv_relay(q, band_at(1), -1)
        kv_pass(4, p, band_at(-1))
        kv_pass(5, q, band_at(1))
        if p == 0:
            for h in range(2):
                w_far(h)
            for h in range(2):
                w_second(h, 0)
            kv_wait(3, 0, sibling, PIECES)
            outer(sibling)
    for s in range(1, 4):
        for h in range(2):
            w_second(h, s)
    for p, q in ((2, 0), (3, 1)):
        kv_wait(0, p, band_at(-1))
        kv_pass(4, p, band_at(-1))
        kv_wait(1, q, band_at(1))
        kv_pass(5, q, band_at(1))
    outer(band_at(-1))
    outer(band_at(1))
    for p in range(PIECES):
        kv_wait(4, p, sibling_at(-1))
        kv_wait(5, p, sibling_at(1))
    outer(sibling_at(-1))
    outer(sibling_at(1))
    for p in (0, 2, 1, 3):
        kv_wait(2, p, band_at(2))
        kv_pass(6, p, band_at(2))
    outer(band_at(2))
    for p in (0, 2, 1, 3):
        kv_wait(6, p, sibling_at(2))
    outer(sibling_at(2))

    def coord(axis):
        return shard % ring if axis == "x" else shard // ring

    def owner(h, one, two):
        return two * ring + one if firsts[h] == "x" else one * ring + two

    def term1(h, one, k, upper):
        slot = owner(h, one, k // hq) * cap + hc * h + upper * hq + k % hq
        return terms[slot_place[slot]]

    n1 = ring * hq
    kinds = {M_R: (2, 0, 1), M_L: (2, 1, -1), O_R: (1, 1, 1), O_L: (-1, 0, -1), C_R: (1, 0, 1), C_L: (-1, 1, -1)}

    def rs_copy(phase, h, kind):
        axis = (firsts if phase == 0 else seconds)[h]
        src, dst = ((send1, recv1), (send2, recv2))[phase]
        return remote(
            src.at[h, kind], dst.at[h, kind], rs_send.at[phase, h, kind], rs_recv.at[phase, h, kind],
            near(axis, kinds[kind][2]),
        )

    def first_send(h, kind):
        by, upper, _ = kinds[kind]
        one = (coord(firsts[h]) + by + ring) % ring
        buf = send1.at[h, kind]
        if kind in (C_R, C_L):
            got = recv1.at[h, M_R if kind == C_R else M_L]
            rs_copy(0, h, M_R if kind == C_R else M_L).wait_recv()

        def block(k, carry):
            value = term1(h, one, k, upper)
            if kind in (C_R, C_L):
                value = value + decode(got, n1, k, side)
            encode(buf, n1, k, value)
            return carry

        lax.fori_loop(0, n1, block, 0)
        go(rs_copy(0, h, kind))

    for kind in (M_R, M_L, O_R, O_L, C_R, C_L):
        for h in range(2):
            first_send(h, kind)

    for h in range(2):
        for s in range(4):
            w_last(h, s)
    local[2].wait()
    wg[wg.shape[0] - 1] = jnp.zeros((side, side), wg.dtype)

    def fill(i, carry):
        for j in range(col_blocks):
            place = i * col_blocks + j
            dense[pl.ds(pl.multiple_of(i * side, side), side), j * side:(j + 1) * side] = wg[place_slot[place]]
        return carry

    lax.fori_loop(0, rows, fill, 0)

    def product(i, carry):
        at = pl.ds(pl.multiple_of(i * 2 * side, 2 * side), 2 * side)
        acc = jnp.zeros((tokens, 2 * side), jnp.float32)
        for b in range(groups):
            acc = acc + lax.dot_general(
                kvg[b], dense[at, b * cols:(b + 1) * cols], (((1,), (1,)), ((), ())),
                preferred_element_type=jnp.float32,
            )
        grad_out[:, at] = acc.astype(grad_out.dtype)
        return carry

    lax.fori_loop(0, rows // 2, product, 0)
    out_copy = pltpu.make_async_copy(grad_out, input_grad, local_sem.at[3])
    out_copy.start()

    for h in range(2):
        for kind in (O_R, O_L, C_R, C_L):
            rs_copy(0, h, kind).wait_recv()
        one = coord(firsts[h])

        def add(k, carry):
            for upper in range(2):
                pair = (C_R, O_L) if upper == 0 else (C_L, O_R)
                value = term1(h, one, k, upper)
                for kind in pair:
                    value = value + decode(recv1.at[h, kind], n1, k, side)
                part[h, (k // hq) * hc + upper * hq + k % hq] = value
            return carry

        lax.fori_loop(0, n1, add, 0)

    def second_send(h, kind):
        by, upper, _ = kinds[kind]
        two = (coord(seconds[h]) + by + ring) % ring
        if kind in (C_R, C_L):
            got = recv2.at[h, M_R if kind == C_R else M_L]
            rs_copy(1, h, M_R if kind == C_R else M_L).wait_recv()
        for k in range(hq):
            value = part[h, two * hc + upper * hq + k]
            if kind in (C_R, C_L):
                value = value + decode(got, hq, k, side)
            encode(send2.at[h, kind], hq, k, value)
        go(rs_copy(1, h, kind))

    for kind in (M_R, M_L, O_R, O_L, C_R, C_L):
        for h in range(2):
            second_send(h, kind)
    for h in range(2):
        two = coord(seconds[h])
        for kind in (O_R, O_L, C_R, C_L):
            rs_copy(1, h, kind).wait_recv()
        for upper in range(2):
            pair = (C_R, O_L) if upper == 0 else (C_L, O_R)
            for k in range(hq):
                value = part[h, two * hc + upper * hq + k]
                for kind in pair:
                    value = value + decode(recv2.at[h, kind], hq, k, side)
                total[hc * h + upper * hq + k] = value

    zq = cap // 4

    def z_copy(phase, d):
        src = zsend1.at[d - 1] if phase == 0 else zsend2
        dst = (zrecv1, zrecv2)[phase].at[d - 1]
        return remote(src, dst, z_send.at[phase, d - 1], z_recv.at[phase, d - 1], {"replica": (rep + d) % 4})

    for d in (2, 1, 3):
        for k in range(zq):
            encode(zsend1.at[d - 1], zq, k, total[(rep + d) % 4 * zq + k])
        go(z_copy(0, d))
    for d in (1, 2, 3):
        z_copy(0, d).wait_recv()
    for k in range(zq):
        value = total[rep * zq + k]
        for d in (1, 2, 3):
            value = value + decode(zrecv1.at[d - 1], zq, k, side)
        encode(zsend2, zq, k, value)
    for d in (2, 1, 3):
        go(z_copy(1, d))

    def put(buf, who):
        for k in range(zq):
            slot = who * zq + k
            value = decode(buf, zq, k, side)
            weight_grad[0, slot] = jnp.where(slot < shard_counts[0, shard], value, 0.0)

    put(zsend2, rep)
    for d in (1, 2, 3):
        z_copy(1, d).wait_recv()
        put(zrecv2.at[d - 1], (rep - d + 4) % 4)
    out_copy.wait()
    for copy in sent:
        copy.wait_send()


def body(inputs, kv_grad, weight_blocks, bitmap, counts):
    side = weight_blocks.shape[-1]
    cap = weight_blocks.shape[1]
    shards = counts.shape[1]
    slots = shards * cap
    tokens, width = inputs.shape
    cols = kv_grad.shape[1]
    places = bitmap.size
    groups = 8

    bits = bitmap.reshape(-1)
    ids = jnp.arange(places, dtype=jnp.int32)
    rank = jnp.sum(jnp.where(ids[None, :] < ids[:, None], bits[None, :], 0), axis=1)
    ends = jnp.cumsum(counts[0])
    passed = ends[None, :] <= rank[:, None]
    holder = jnp.sum(passed.astype(jnp.int32), axis=1)
    start = jnp.max(jnp.where(passed, ends[None, :], 0), axis=1)
    place_slot = jnp.where(bits == 1, holder * cap + rank - start, slots)
    slot_ids = jnp.arange(slots, dtype=jnp.int32)
    slot_place = jnp.sum(jnp.where(place_slot[None, :] == slot_ids[:, None], ids[None, :], 0), axis=1)

    n1, n2 = cap, cap // 4
    half = side // 2
    big, small = n1 * half + 8, n2 * half + 8
    anywhere = pl.BlockSpec(memory_space=pl.ANY)
    scalars = pl.BlockSpec(memory_space=pltpu.SMEM)
    return pl.pallas_call(
        kernel,
        out_shape=(
            jax.ShapeDtypeStruct(inputs.shape, jnp.bfloat16),
            jax.ShapeDtypeStruct(weight_blocks.shape, jnp.float32),
        ),
        in_specs=[scalars, scalars, scalars, anywhere, anywhere, anywhere],
        out_specs=(anywhere, pl.BlockSpec(memory_space=pltpu.VMEM)),
        scratch_shapes=[
            pltpu.VMEM((tokens, width), jnp.bfloat16),
            pltpu.VMEM((width, tokens), jnp.bfloat16),
            pltpu.VMEM((groups, tokens, cols), jnp.bfloat16),
            pltpu.VMEM((slots + 1, side, side), jnp.bfloat16),
            pltpu.VMEM((width, groups * cols), jnp.bfloat16),
            pltpu.VMEM((places, side, side), jnp.float32),
            pltpu.VMEM((tokens, width), jnp.bfloat16),
            pltpu.VMEM((2, 2 * cap, side, side), jnp.float32),
            pltpu.VMEM((cap, side, side), jnp.float32),
            pltpu.VMEM((2, 6, big, side), jnp.int32),
            pltpu.VMEM((2, 6, big, side), jnp.int32),
            pltpu.VMEM((2, 6, small, side), jnp.int32),
            pltpu.VMEM((2, 6, small, side), jnp.int32),
            pltpu.VMEM((3, small, side), jnp.int32),
            pltpu.VMEM((3, small, side), jnp.int32),
            pltpu.VMEM((small, side), jnp.int32),
            pltpu.VMEM((3, small, side), jnp.int32),
            pltpu.SemaphoreType.DMA((4,)),
            pltpu.SemaphoreType.DMA((7, PIECES)),
            pltpu.SemaphoreType.DMA((7, PIECES)),
            pltpu.SemaphoreType.DMA((2, 10, 2)),
            pltpu.SemaphoreType.DMA((2, 10, 2)),
            pltpu.SemaphoreType.DMA((2, 2, 6)),
            pltpu.SemaphoreType.DMA((2, 2, 6)),
            pltpu.SemaphoreType.DMA((2, 3)),
            pltpu.SemaphoreType.DMA((2, 3)),
        ],
        compiler_params=pltpu.CompilerParams(
            collective_id=0, has_side_effects=True, vmem_limit_bytes=48 * 1024 * 1024
        ),
    )(slot_place, place_slot, counts, inputs, kv_grad, weight_blocks)


def solution(mesh):
    in_specs = (
        P(("replica", "fsdp"), "tensor"),
        P(("replica", "fsdp"), "tensor"),
        P("tensor", "fsdp", None, None),
        P("tensor", None),
        P("tensor", None),
    )
    out_specs = (P(("replica", "fsdp"), "tensor"), P("tensor", "fsdp", None, None))
    return jax.shard_map(body, mesh=mesh, in_specs=in_specs, out_specs=out_specs, check_vma=False)
```

time: 435 us -> 106 us (0.24)
  the two profiles are of different devices: /device:TPU:2 before, /device:TPU:4 now
where the time goes in v1:
time: 106 us
  Pallas kernels  98.2 us (93%)
  local copies, waits for them, and re-layouts  6.29 us (6%)
    pallas_call x1, Pallas kernels, body(): pl.pallas_call(kernel, out_shape=(jax.ShapeDtypeStruct(inputs.shape, jnp....  98.2 us
    unnamed x10, local copies, waits for them, and re-layouts  5.44 us

profile of v1, /device:TPU:4, one launch (start us, length us, event | category | flops | bytes accessed | tf_op | source)
XLA Modules:
  0.0 105.6 jit_solution(15997161513270114860)
XLA Ops:
  0.6 0.8 reshape.48
  1.4 0.0 copy-start.3
  1.4 0.1 select_reduce_fusion.1
  1.5 0.5 copy-done.3
  2.1 0.1 copy.9
  2.2 0.1 reduce
  2.3 0.1 fusion
  2.4 0.1 select_reduce_fusion.slot_place
  2.5 0.0 copy-start
  2.5 1.2 %copy-done = bf16[512,1024]{1,0:T(8,128)(2,1)S(1)} copy-done((bf16[512,1024]{1,0:T(8,128)(2,1)S(1)}, bf16[512,1024]{1,0:T(8,128)(2,1)}, u32[]{:S(2)}) %copy-start) | copy-done | bytes 1048600
  3.7 0.0 copy-start.1
  3.7 0.9 copy-done.1
  4.7 0.0 copy-start.2
  4.7 0.9 copy-done.2
  5.6 98.2 %shard_map.68 = (bf16[512,1024]{1,0:T(8,128)(2,1)S(1)}, f32[1,8,128,128]{3,2,1,0:T(8,128)S(1)}) custom-call(s32[128]{0:T(128)S(1)} %select_reduce_fusion.slot_place, s32[128]{0:T(128)S(1)} %compare_select_fusion.1.place_slot, s32[1,16]{1,0:T(1,128)S(1)} %copy-done.3, bf16[512,1024]{1,0:T(8,128)(2,1)S(1)} %copy-done, bf16[512,256]{1,0:T(8,128)(2,1)S(1)} %copy-done.1, ...), custom_call_target="tpu_custom_call" | custom-call | tf_op jit(solution)/shard_map/pallas_call | solution.py:403
  103.8 1.0 copy.12
  104.8 0.8 copy.13
  (2 shorter events, 0.0 us)
Async XLA Ops:
  1.4 0.7 copy-start.3
  2.5 1.2 %copy-start = (bf16[512,1024]{1,0:T(8,128)(2,1)S(1)}, bf16[512,1024]{1,0:T(8,128)(2,1)}, u32[]{:S(2)}) copy-start(bf16[512,1024]{1,0:T(8,128)(2,1)} %inputs.1) | copy-start | bytes 3145732
  3.7 0.9 copy-start.1
  4.7 0.9 copy-start.2

commit v2 on v1

v2 whole, which is shorter than its diff:
```python
import functools

import jax
import jax.numpy as jnp
from jax import lax
from jax.experimental import pallas as pl
from jax.experimental.pallas import tpu as pltpu
from jax.sharding import PartitionSpec as P

MESH = pl.DeviceIdType.MESH
RADIUS = 32700.0
STEPS = 16.0
LIFT = 2048.0
PIECES = 4
WAVES = ((0, 64), (64, 64))
M_R, M_L, O_R, O_L, C_R, C_L = range(6)


def encode(buf, count, k, block):
    half = block.shape[0] // 2
    peak = jnp.maximum(jnp.max(jnp.abs(block), axis=0, keepdims=True), 1e-30)
    code = (jnp.log(peak) * STEPS + LIFT).astype(jnp.int32) + 1
    scale = jnp.exp((code.astype(jnp.float32) - LIFT) * (1.0 / STEPS))
    whole = jnp.round(block * (RADIUS / scale)).astype(jnp.int32)
    buf[pl.ds(k * half, half), :] = whole[:half] * 65536 + whole[half:]
    buf[pl.ds(count * half + k, 1), :] = code


def decode(buf, count, k, height):
    half = height // 2
    pair = buf[pl.ds(k * half, half), :]
    code = buf[pl.ds(count * half + k, 1), :]
    scale = jnp.exp((code.astype(jnp.float32) - LIFT) * (1.0 / STEPS)) * (1.0 / RADIUS)
    low = (pair << 16) >> 16
    high = (pair - low) >> 16
    return jnp.concatenate([high.astype(jnp.float32), low.astype(jnp.float32)], axis=0) * scale


def number(bitmap, counts, cap):
    (height, width), shards = bitmap.shape, counts.shape[1]
    places = height * width

    def ids(shape, axis):
        return lax.broadcasted_iota(jnp.int32, shape, axis)

    spread = (ids((width, places), 1) % width == ids((width, places), 0)).astype(jnp.float32)
    wide = jnp.dot(bitmap.astype(jnp.float32), spread, preferred_element_type=jnp.float32)
    mine = ids((height, places), 1) // width == ids((height, places), 0)
    bits = jnp.sum(jnp.where(mine, wide, 0.0), axis=0, keepdims=True)
    before = (ids((places, places), 0) < ids((places, places), 1)).astype(jnp.float32)
    rank = jnp.dot(jnp.broadcast_to(bits, (height, places)), before, preferred_element_type=jnp.float32)[:1]
    square = (shards, shards)
    upto = ids(square, 1) <= ids(square, 0)
    ends = jnp.sum(jnp.where(upto, jnp.broadcast_to(counts, square).astype(jnp.float32), 0.0), axis=1, keepdims=True)
    passed = ends <= rank
    holder = jnp.sum(jnp.where(passed, 1.0, 0.0), axis=0, keepdims=True)
    start = jnp.max(jnp.where(passed, ends, 0.0), axis=0, keepdims=True)
    place_slot = jnp.where(bits > 0.5, holder * cap + rank - start, float(shards * cap))
    large = (places, places)
    down = jnp.sum(jnp.where(ids(large, 0) == ids(large, 1), place_slot, 0.0), axis=1, keepdims=True)
    held = down == ids(large, 1).astype(jnp.float32)
    slot_place = jnp.sum(jnp.where(held, ids(large, 0).astype(jnp.float32), 0.0), axis=0, keepdims=True)
    row = ids((8, places), 0)
    found = jnp.where(row == 0, slot_place, jnp.where(row == 1, place_slot, 0.0)).astype(jnp.int32)
    return jnp.clip(found, 0, jnp.where(row == 0, places - 1, shards * cap))


def kernel(
    shard_counts, inputs, kv_grad, weights, bitmap, counts,
    input_grad, weight_grad,
    bits_in, counts_in, tables, table, x_in, x_turned, kvg, wg, dense, terms, part, total,
    send1, recv1, send2, recv2, zsend1, zrecv1, zsend2, zrecv2,
    local_sem, kv_send, kv_recv, w_send, w_recv, rs_send, rs_recv, z_send, z_recv,
):
    rep = lax.axis_index("replica")
    shard = lax.axis_index("fsdp")
    band = lax.axis_index("tensor")
    tokens, width = x_in.shape
    side = terms.shape[-1]
    cap = weights.shape[1]
    cols = kv_grad.shape[1]
    hc = cap // 2
    ring = 4
    rows, groups = width // side, 8
    col_blocks = cols // side * groups
    piece = tokens // PIECES

    def shift(f, axis, by):
        y, x = f // ring, f % ring
        if axis == "x":
            return y * ring + (x + by + ring) % ring
        return ((y + by + ring) % ring) * ring + x

    def near(axis, by):
        return {"fsdp": shift(shard, axis, by)}

    def band_at(by):
        return (band + 2 * by + groups) % groups

    sibling = band + 1 - 2 * (band % 2)

    def sibling_at(by):
        return (sibling + 2 * by + groups) % groups

    def remote(src, dst, send_sem, recv_sem, where):
        return pltpu.make_async_remote_copy(
            src_ref=src, dst_ref=dst, send_sem=send_sem, recv_sem=recv_sem,
            device_id=where, device_id_type=MESH,
        )

    partners = [{"tensor": sibling}, {"tensor": band_at(1)}, {"tensor": band_at(-1)}]
    partners += [near(axis, by) for axis in ("x", "y") for by in (1, -1)]
    partners += [{"replica": (rep + d) % 4} for d in (1, 2, 3)]
    barrier = pltpu.get_barrier_semaphore()
    for where in partners:
        pl.semaphore_signal(barrier, inc=1, device_id=where, device_id_type=MESH)
    pl.semaphore_wait(barrier, len(partners))

    sent = []

    def go(copy):
        copy.start()
        sent.append(copy)

    def kv_at(b, p, n=1):
        return kvg.at[b, pl.ds(p * piece, n * piece), :]

    own_kv = [kv_grad.at[pl.ds(p * piece, piece), :] for p in range(PIECES)]
    right_order = list(range(PIECES))
    left_order = right_order[PIECES // 2:] + right_order[:PIECES // 2]
    for a, b in zip(right_order, left_order):
        go(remote(own_kv[a], kv_at(band, a), kv_send.at[0, a], kv_recv.at[0, a], {"tensor": band_at(1)}))
        go(remote(own_kv[b], kv_at(band, b), kv_send.at[1, b], kv_recv.at[1, b], {"tensor": band_at(-1)}))

    firsts = ("x", "y")
    seconds = ("y", "x")

    def w_at(f, slot, n):
        return wg.at[pl.ds(f * cap + slot, n)]

    for h in range(2):
        own_w = weights.at[0, pl.ds(hc * h, hc)]
        for d, by in ((0, 1), (1, -1)):
            go(remote(own_w, w_at(shard, hc * h, hc), w_send.at[h, 0, d], w_recv.at[h, 0, d], near(firsts[h], by)))
            go(remote(own_w, w_at(shard, hc * h, hc), w_send.at[h, 2, d], w_recv.at[h, 2, d], near(seconds[h], by)))
    go(remote(kv_grad, kv_at(band, 0, PIECES), kv_send.at[3, 0], kv_recv.at[3, 0], {"tensor": sibling}))
    local = [
        pltpu.make_async_copy(inputs, x_in, local_sem.at[0]),
        pltpu.make_async_copy(kv_grad, kvg.at[band], local_sem.at[1]),
        pltpu.make_async_copy(weights.at[0], w_at(shard, 0, cap), local_sem.at[2]),
        pltpu.make_async_copy(bitmap, bits_in, local_sem.at[3]),
        pltpu.make_async_copy(counts, counts_in, local_sem.at[4]),
    ]
    for copy in local:
        copy.start()

    def kv_wait(which, p, b, n=1):
        remote(kv_at(b, p, n), kv_at(b, p, n), kv_send.at[which, p], kv_recv.at[which, p], {"tensor": sibling}).wait_recv()

    def kv_pass(which, p, b):
        go(remote(kv_at(b, p), kv_at(b, p), kv_send.at[which, p], kv_recv.at[which, p], {"tensor": sibling}))

    def kv_relay(p, b, by):
        go(remote(kv_at(b, p), kv_at(b, p), kv_send.at[2, p], kv_recv.at[2, p], {"tensor": band_at(by)}))

    def w_wait(h, which, d, f, slot, n):
        at = w_at(f, hc * h + slot, n)
        remote(at, at, w_send.at[h, which, d], w_recv.at[h, which, d], {"tensor": sibling}).wait_recv()

    def w_go(h, which, d, f, slot, n, axis):
        at = w_at(f, hc * h + slot, n)
        go(remote(at, at, w_send.at[h, which, d], w_recv.at[h, which, d], near(axis, 1 if d == 0 else -1)))

    hq = hc // 2

    def w_first(h):
        for d, by in ((0, -1), (1, 1)):
            src = shift(shard, firsts[h], by)
            w_wait(h, 0, d, src, 0, hc)
            w_go(h, 1, d, src, d * hq, hq, firsts[h])
            for e in range(2):
                w_go(h, 3 + d, e, src, 0, hc, seconds[h])

    def w_far(h):
        src = shift(shard, firsts[h], 2)
        for d in range(2):
            w_wait(h, 1, d, src, d * hq, hq)
        for e in range(2):
            w_go(h, 5, e, src, 0, hc, seconds[h])

    def w_second(h, s):
        for d, by in ((0, -1), (1, 1)):
            src = shift(shift(shard, firsts[h], (0, -1, 1, 2)[s]), seconds[h], by)
            w_wait(h, 2 + s, d, src, 0, hc)
            w_go(h, 6 + s, d, src, d * hq, hq, seconds[h])

    def w_last(h, s):
        src = shift(shift(shard, firsts[h], (0, -1, 1, 2)[s]), seconds[h], 2)
        for d in range(2):
            w_wait(h, 6 + s, d, src, d * hq, hq)

    def outer(b):
        def tile(i, carry):
            at = pl.ds(pl.multiple_of(i * 2 * side, 2 * side), 2 * side)
            got = jnp.dot(x_turned[at, :], kvg[b], preferred_element_type=jnp.float32)
            for u in range(2):
                for v in range(2):
                    place = (2 * i + u) * col_blocks + 2 * b + v
                    terms[place] = got[u * side:(u + 1) * side, v * side:(v + 1) * side]
            return carry

        lax.fori_loop(0, rows // 2, tile, 0)

    local[3].wait()
    local[4].wait()
    tables[...] = number(bits_in[...], counts_in[...], cap)
    to_scalars = pltpu.make_async_copy(tables, table, local_sem.at[5])
    to_scalars.start()
    local[0].wait()
    local[1].wait()
    x_turned[...] = x_in[...].T
    for h in range(2):
        w_first(h)
    outer(band)
    to_scalars.wait()
    for p, q in ((0, 2), (1, 3)):
        kv_wait(0, p, band_at(-1))
        kv_relay(p, band_at(-1), 1)
        kv_wait(1, q, band_at(1))
        kv_relay(q, band_at(1), -1)
        kv_pass(4, p, band_at(-1))
        kv_pass(5, q, band_at(1))
        if p == 0:
            for h in range(2):
                w_far(h)
            for h in range(2):
                w_second(h, 0)
            kv_wait(3, 0, sibling, PIECES)
            outer(sibling)
    for s in range(1, 4):
        for h in range(2):
            w_second(h, s)
    for p, q in ((2, 0), (3, 1)):
        kv_wait(0, p, band_at(-1))
        kv_pass(4, p, band_at(-1))
        kv_wait(1, q, band_at(1))
        kv_pass(5, q, band_at(1))
    outer(band_at(-1))
    outer(band_at(1))
    for p in range(PIECES):
        kv_wait(4, p, sibling_at(-1))
        kv_wait(5, p, sibling_at(1))
    outer(sibling_at(-1))
    outer(sibling_at(1))
    for h in range(2):
        for s in range(4):
            w_last(h, s)
    local[2].wait()
    wg[wg.shape[0] - 1] = jnp.zeros((side, side), wg.dtype)

    def fill(i, carry):
        for j in range(col_blocks):
            place = i * col_blocks + j
            dense[pl.ds(pl.multiple_of(i * side, side), side), j * side:(j + 1) * side] = wg[jnp.clip(table[1, place], 0, wg.shape[0] - 1)]
        return carry

    lax.fori_loop(0, rows, fill, 0)
    for p in (0, 2, 1, 3):
        kv_wait(2, p, band_at(2))
        kv_pass(6, p, band_at(2))
    outer(band_at(2))
    for p in (0, 2, 1, 3):
        kv_wait(6, p, sibling_at(2))
    outer(sibling_at(2))

    n1 = ring * hq

    def coord(axis):
        return shard % ring if axis == "x" else shard // ring

    def owner(h, one, two):
        return two * ring + one if firsts[h] == "x" else one * ring + two

    def term1(w, h, one, k, upper):
        slot = owner(h, one, k // hq) * cap + hc * h + upper * hq + k % hq
        return terms[jnp.clip(table[0, slot], 0, terms.shape[0] - 1), pl.ds(WAVES[w][0], WAVES[w][1]), :]

    def tall(w, blocks):
        return pl.ds(0, blocks * WAVES[w][1] // 2 + 8)

    def own_part(w, h, two, upper, k):
        return part[w, h, two * hc + upper * hq + k, pl.ds(0, WAVES[w][1]), :]

    kinds = {M_R: (2, 0, 1), M_L: (2, 1, -1), O_R: (1, 1, 1), O_L: (-1, 0, -1), C_R: (1, 0, 1), C_L: (-1, 1, -1)}

    def rs_copy(phase, w, h, kind):
        axis = (firsts if phase == 0 else seconds)[h]
        src, dst = ((send1, recv1), (send2, recv2))[phase]
        blocks = (n1, hq)[phase]
        return remote(
            src.at[w, h, kind, tall(w, blocks)], dst.at[w, h, kind, tall(w, blocks)], rs_send.at[phase, w, h, kind], rs_recv.at[phase, w, h, kind],
            near(axis, kinds[kind][2]),
        )

    def first_send(w, pair):
        for kind in pair:
            for h in range(2):
                by, upper, _ = kinds[kind]
                one = (coord(firsts[h]) + by + ring) % ring
                relayed = {C_R: M_R, C_L: M_L}.get(kind)
                if relayed is not None:
                    rs_copy(0, w, h, relayed).wait_recv()

                for k in range(n1):
                    value = term1(w, h, one, k, upper)
                    if relayed is not None:
                        value = value + decode(recv1.at[w, h, relayed], n1, k, WAVES[w][1])
                    encode(send1.at[w, h, kind], n1, k, value)
                go(rs_copy(0, w, h, kind))

    def first_sum(w):
        for h in range(2):
            for kind in (O_R, O_L, C_R, C_L):
                rs_copy(0, w, h, kind).wait_recv()
            one = coord(firsts[h])

            for k in range(n1):
                for upper, pair in ((0, (C_R, O_L)), (1, (C_L, O_R))):
                    value = term1(w, h, one, k, upper)
                    for kind in pair:
                        value = value + decode(recv1.at[w, h, kind], n1, k, WAVES[w][1])
                    part[w, h, (k // hq) * hc + upper * hq + k % hq, pl.ds(0, WAVES[w][1]), :] = value

    def second_send(w, pair):
        relay = {C_R: M_R, C_L: M_L}
        both = [(kind, h) for kind in pair for h in range(2)]
        for kind, h in both:
            if kind in relay:
                rs_copy(1, w, h, relay[kind]).wait_recv()
        for kind, h in both:
            by, upper, _ = kinds[kind]
            two = (coord(seconds[h]) + by + ring) % ring
            for k in range(hq):
                value = own_part(w, h, two, upper, k)
                if kind in relay:
                    value = value + decode(recv2.at[w, h, relay[kind]], hq, k, WAVES[w][1])
                encode(send2.at[w, h, kind], hq, k, value)
        for kind, h in both:
            go(rs_copy(1, w, h, kind))

    def second_sum(w):
        for h in range(2):
            for kind in (O_R, O_L, C_R, C_L):
                rs_copy(1, w, h, kind).wait_recv()
        for h in range(2):
            two = coord(seconds[h])
            for upper, pair in ((0, (C_R, O_L)), (1, (C_L, O_R))):
                for k in range(hq):
                    value = own_part(w, h, two, upper, k)
                    for kind in pair:
                        value = value + decode(recv2.at[w, h, kind], hq, k, WAVES[w][1])
                    total[hc * h + upper * hq + k, pl.ds(WAVES[w][0], WAVES[w][1]), :] = value

    zq = cap // 4

    def z_copy(phase, w, d):
        src = zsend1.at[w, d - 1, tall(w, zq)] if phase == 0 else zsend2.at[w, tall(w, zq)]
        dst = (zrecv1, zrecv2)[phase].at[w, d - 1, tall(w, zq)]
        return remote(src, dst, z_send.at[phase, w, d - 1], z_recv.at[phase, w, d - 1], {"replica": (rep + d) % 4})

    def summed(w, who, k):
        return total[who * zq + k, pl.ds(WAVES[w][0], WAVES[w][1]), :]

    def z_scatter(w):
        for d in (2, 1, 3):
            for k in range(zq):
                encode(zsend1.at[w, d - 1], zq, k, summed(w, (rep + d) % 4, k))
        for d in (2, 1, 3):
            go(z_copy(0, w, d))

    def put(buf, w, who):
        for k in range(zq):
            slot = who * zq + k
            value = decode(buf, zq, k, WAVES[w][1])
            weight_grad[0, slot, pl.ds(WAVES[w][0], WAVES[w][1]), :] = jnp.where(slot < shard_counts[0, shard], value, 0.0)

    def z_hand(w):
        for d in (1, 3, 2):
            z_copy(0, w, d).wait_recv()
        for k in range(zq):
            value = summed(w, rep, k)
            for d in (1, 3, 2):
                value = value + decode(zrecv1.at[w, d - 1], zq, k, WAVES[w][1])
            encode(zsend2.at[w], zq, k, value)
        for d in (2, 1, 3):
            go(z_copy(1, w, d))
        put(zsend2.at[w], w, rep)

    def z_take(w):
        for d in (1, 3, 2):
            z_copy(1, w, d).wait_recv()
        for d in (1, 3, 2):
            put(zrecv2.at[w, d - 1], w, (rep - d + 4) % 4)

    def product(i, carry):
        at = pl.ds(pl.multiple_of(i * 2 * side, 2 * side), 2 * side)
        acc = jnp.zeros((tokens, 2 * side), jnp.float32)
        for b in range(groups):
            acc = acc + lax.dot_general(
                kvg[b], dense[at, b * cols:(b + 1) * cols], (((1,), (1,)), ((), ())),
                preferred_element_type=jnp.float32,
            )
        input_grad[:, at] = acc.astype(input_grad.dtype)
        return carry

    early, alone, late = (M_R, M_L), (O_R, O_L), (C_R, C_L)
    first_send(0, early)
    first_send(0, alone)
    first_send(0, late)
    first_send(1, early)
    first_send(1, alone)
    first_sum(0)
    second_send(0, early)
    second_send(0, alone)
    first_send(1, late)
    second_send(0, late)
    first_sum(1)
    second_send(1, early)
    second_send(1, alone)
    second_sum(0)
    z_scatter(0)
    second_send(1, late)
    z_hand(0)
    second_sum(1)
    z_scatter(1)
    lax.fori_loop(0, rows // 2, product, 0)
    z_take(0)
    z_hand(1)
    z_take(1)
    for copy in sent:
        copy.wait_send()


def body(inputs, kv_grad, weight_blocks, bitmap, counts):
    side = weight_blocks.shape[-1]
    cap = weight_blocks.shape[1]
    shards = counts.shape[1]
    slots = shards * cap
    tokens, width = inputs.shape
    cols = kv_grad.shape[1]
    places = bitmap.size
    groups = 8
    waves, half = len(WAVES), max(n for _, n in WAVES) // 2
    big, small = cap * half + 8, cap // 4 * half + 8
    held = pl.BlockSpec(memory_space=pltpu.HBM)
    fast = pl.BlockSpec(memory_space=pltpu.VMEM)
    scalars = pl.BlockSpec(memory_space=pltpu.SMEM)
    return pl.pallas_call(
        kernel,
        out_shape=(
            jax.ShapeDtypeStruct(inputs.shape, jnp.bfloat16),
            jax.ShapeDtypeStruct(weight_blocks.shape, jnp.float32),
        ),
        in_specs=[scalars, held, held, held, held, held],
        out_specs=(fast, fast),
        scratch_shapes=[
            pltpu.VMEM(bitmap.shape, jnp.int32),
            pltpu.VMEM(counts.shape, jnp.int32),
            pltpu.VMEM((8, places), jnp.int32),
            pltpu.SMEM((8, places), jnp.int32),
            pltpu.VMEM((tokens, width), jnp.bfloat16),
            pltpu.VMEM((width, tokens), jnp.bfloat16),
            pltpu.VMEM((groups, tokens, cols), jnp.bfloat16),
            pltpu.VMEM((slots + 1, side, side), jnp.bfloat16),
            pltpu.VMEM((width, groups * cols), jnp.bfloat16),
            pltpu.VMEM((places, side, side), jnp.float32),
            pltpu.VMEM((waves, 2, 2 * cap, 2 * half, side), jnp.float32),
            pltpu.VMEM((cap, side, side), jnp.float32),
            pltpu.VMEM((waves, 2, 6, big, side), jnp.int32),
            pltpu.VMEM((waves, 2, 6, big, side), jnp.int32),
            pltpu.VMEM((waves, 2, 6, small, side), jnp.int32),
            pltpu.VMEM((waves, 2, 6, small, side), jnp.int32),
            pltpu.VMEM((waves, 3, small, side), jnp.int32),
            pltpu.VMEM((waves, 3, small, side), jnp.int32),
            pltpu.VMEM((waves, small, side), jnp.int32),
            pltpu.VMEM((waves, 3, small, side), jnp.int32),
            pltpu.SemaphoreType.DMA((6,)),
            pltpu.SemaphoreType.DMA((7, PIECES)),
            pltpu.SemaphoreType.DMA((7, PIECES)),
            pltpu.SemaphoreType.DMA((2, 10, 2)),
            pltpu.SemaphoreType.DMA((2, 10, 2)),
            pltpu.SemaphoreType.DMA((2, waves, 2, 6)),
            pltpu.SemaphoreType.DMA((2, waves, 2, 6)),
            pltpu.SemaphoreType.DMA((2, waves, 3)),
            pltpu.SemaphoreType.DMA((2, waves, 3)),
        ],
        compiler_params=pltpu.CompilerParams(
            collective_id=0, has_side_effects=True, vmem_limit_bytes=48 * 1024 * 1024
        ),
    )(counts, *(pltpu.with_memory_space_constraint(a, pltpu.HBM) for a in (inputs, kv_grad, weight_blocks, bitmap, counts)))


def solution(mesh):
    in_specs = (
        P(("replica", "fsdp"), "tensor"),
        P(("replica", "fsdp"), "tensor"),
        P("tensor", "fsdp", None, None),
        P("tensor", None),
        P("tensor", None),
    )
    out_specs = (P(("replica", "fsdp"), "tensor"), P("tensor", "fsdp", None, None))
    return jax.shard_map(body, mesh=mesh, in_specs=in_specs, out_specs=out_specs, check_vma=False)
```

time: 106 us -> 99.1 us (0.935)
  the two profiles are of different devices: /device:TPU:4 before, /device:TPU:32 now
where the time goes in v2:
time: 99.1 us; the launch traced here: 98.9 us
  Pallas kernels  96.5 us (97%)
  local copies, waits for them, and re-layouts  1.77 us (2%)
    pallas_call x1, Pallas kernels, body(): pl.pallas_call(kernel, out_shape=(jax.ShapeDtypeStruct(inputs.shape, jnp....  96.5 us

profile of v2, /device:TPU:32, one launch (start us, length us, event | category | flops | bytes accessed | tf_op | source)
XLA Modules:
  0.0 98.9 jit_solution(971586737139859952)
XLA Ops:
  0.6 96.5 %shard_map.68 = (bf16[512,1024]{1,0:T(8,128)(2,1)S(1)}, f32[1,8,128,128]{3,2,1,0:T(8,128)S(1)}) custom-call(s32[1,16]{1,0:T(1,128)} %counts.1, bf16[512,1024]{1,0:T(8,128)(2,1)} %inputs.1, bf16[512,256]{1,0:T(8,128)(2,1)} %kv_grad.1, bf16[1,8,128,128]{3,2,1,0:T(8,128)(2,1)} %weights.1, s32[8,16]{1,0:T(8,128)} %bitmap.1, s32[1,16]{1,0:T(1,128)} %counts.1), custom_call_target="tpu_custom_call" | custom-call | tf_op jit(solution)/shard_map/pallas_call | solution.py:458
  97.2 1.0 copy.9
  98.1 0.8 copy.10

commit v3 on v2

--- a/solution.py
+++ b/solution.py
@@ -109,7 +109,7 @@
         )
 
     partners = [{"tensor": sibling}, {"tensor": band_at(1)}, {"tensor": band_at(-1)}]
-    partners += [near(axis, by) for axis in ("x", "y") for by in (1, -1)]
+    partners += [near(axis, by) for axis in ("x", "y") for by in (1, -1, 2)]
     partners += [{"replica": (rep + d) % 4} for d in (1, 2, 3)]
     barrier = pltpu.get_barrier_semaphore()
     for where in partners:
@@ -299,7 +299,7 @@
         blocks = (n1, hq)[phase]
         return remote(
             src.at[w, h, kind, tall(w, blocks)], dst.at[w, h, kind, tall(w, blocks)], rs_send.at[phase, w, h, kind], rs_recv.at[phase, w, h, kind],
-            near(axis, kinds[kind][2]),
+            near(axis, kinds[kind][0] if phase == 1 else kinds[kind][2]),
         )
 
     def first_send(w, pair):
@@ -331,33 +331,26 @@
                         value = value + decode(recv1.at[w, h, kind], n1, k, WAVES[w][1])
                     part[w, h, (k // hq) * hc + upper * hq + k % hq, pl.ds(0, WAVES[w][1]), :] = value
 
-    def second_send(w, pair):
-        relay = {C_R: M_R, C_L: M_L}
-        both = [(kind, h) for kind in pair for h in range(2)]
-        for kind, h in both:
-            if kind in relay:
-                rs_copy(1, w, h, relay[kind]).wait_recv()
-        for kind, h in both:
-            by, upper, _ = kinds[kind]
-            two = (coord(seconds[h]) + by + ring) % ring
-            for k in range(hq):
-                value = own_part(w, h, two, upper, k)
-                if kind in relay:
-                    value = value + decode(recv2.at[w, h, relay[kind]], hq, k, WAVES[w][1])
-                encode(send2.at[w, h, kind], hq, k, value)
-        for kind, h in both:
-            go(rs_copy(1, w, h, kind))
+    def second_send(w):
+        for h in range(2):
+            for kind in range(6):
+                by, upper, _ = kinds[kind]
+                two = (coord(seconds[h]) + by + ring) % ring
+                for k in range(hq):
+                    encode(send2.at[w, h, kind], hq, k, own_part(w, h, two, upper, k))
+            for kind in range(6):
+                go(rs_copy(1, w, h, kind))
 
     def second_sum(w):
         for h in range(2):
-            for kind in (O_R, O_L, C_R, C_L):
+            for kind in range(6):
                 rs_copy(1, w, h, kind).wait_recv()
         for h in range(2):
             two = coord(seconds[h])
-            for upper, pair in ((0, (C_R, O_L)), (1, (C_L, O_R))):
+            for upper, three in ((0, (C_R, O_L, M_R)), (1, (C_L, O_R, M_L))):
                 for k in range(hq):
                     value = own_part(w, h, two, upper, k)
-                    for kind in pair:
+                    for kind in three:
                         value = value + decode(recv2.at[w, h, kind], hq, k, WAVES[w][1])
                     total[hc * h + upper * hq + k, pl.ds(WAVES[w][0], WAVES[w][1]), :] = value
 
@@ -419,21 +412,17 @@
     first_send(0, late)
     first_send(1, early)
     first_send(1, alone)
+    lax.fori_loop(0, rows // 2, product, 0)
     first_sum(0)
-    second_send(0, early)
-    second_send(0, alone)
+    second_send(0)
     first_send(1, late)
-    second_send(0, late)
-    first_sum(1)
-    second_send(1, early)
-    second_send(1, alone)
     second_sum(0)
     z_scatter(0)
-    second_send(1, late)
+    first_sum(1)
+    second_send(1)
     z_hand(0)
     second_sum(1)
     z_scatter(1)
-    lax.fori_loop(0, rows // 2, product, 0)
     z_take(0)
     z_hand(1)
     z_take(1)

time: 99.1 us -> 98.3 us (level)
  no operation moved by 1% of the time
where the time goes in v3:
time: 98.3 us; the launch traced here: 98.1 us
  Pallas kernels  95.7 us (97%)
  local copies, waits for them, and re-layouts  1.77 us (2%)
    pallas_call x1, Pallas kernels, body(): pl.pallas_call(kernel, out_shape=(jax.ShapeDtypeStruct(inputs.shape, jnp....  95.7 us

profile of v3, /device:TPU:32, one launch (start us, length us, event | category | flops | bytes accessed | tf_op | source)
XLA Modules:
  0.0 98.1 jit_solution(11680244021072161215)
XLA Ops:
  0.6 95.7 %shard_map.68 = (bf16[512,1024]{1,0:T(8,128)(2,1)S(1)}, f32[1,8,128,128]{3,2,1,0:T(8,128)S(1)}) custom-call(s32[1,16]{1,0:T(1,128)} %counts.1, bf16[512,1024]{1,0:T(8,128)(2,1)} %inputs.1, bf16[512,256]{1,0:T(8,128)(2,1)} %kv_grad.1, bf16[1,8,128,128]{3,2,1,0:T(8,128)(2,1)} %weights.1, s32[8,16]{1,0:T(8,128)} %bitmap.1, s32[1,16]{1,0:T(1,128)} %counts.1), custom_call_target="tpu_custom_call" | custom-call | tf_op jit(solution)/shard_map/pallas_call | solution.py:447
  96.4 1.0 copy.9
  97.3 0.8 copy.10

commit v4 on v3

--- a/solution.py
+++ b/solution.py
@@ -422,7 +422,11 @@
     second_send(1)
     z_hand(0)
     second_sum(1)
+    over = len(sent)
     z_scatter(1)
+    for copy in sent[:over]:
+        copy.wait_send()
+    del sent[:over]
     z_take(0)
     z_hand(1)
     z_take(1)

time: 98.3 us -> 98.1 us (level)
  no operation moved by 1% of the time
where the time goes in v4:
time: 98.1 us; the launch traced here: 97.9 us
  Pallas kernels  95.5 us (97%)
  local copies, waits for them, and re-layouts  1.77 us (2%)
    pallas_call x1, Pallas kernels, body(): pl.pallas_call(kernel, out_shape=(jax.ShapeDtypeStruct(inputs.shape, jnp....  95.5 us

profile of v4, /device:TPU:32, one launch (start us, length us, event | category | flops | bytes accessed | tf_op | source)
XLA Modules:
  0.0 97.9 jit_solution(184087687699002519)
XLA Ops:
  0.6 95.5 %shard_map.68 = (bf16[512,1024]{1,0:T(8,128)(2,1)S(1)}, f32[1,8,128,128]{3,2,1,0:T(8,128)S(1)}) custom-call(s32[1,16]{1,0:T(1,128)} %counts.1, bf16[512,1024]{1,0:T(8,128)(2,1)} %inputs.1, bf16[512,256]{1,0:T(8,128)(2,1)} %kv_grad.1, bf16[1,8,128,128]{3,2,1,0:T(8,128)(2,1)} %weights.1, s32[8,16]{1,0:T(8,128)} %bitmap.1, s32[1,16]{1,0:T(1,128)} %counts.1), custom_call_target="tpu_custom_call" | custom-call | tf_op jit(solution)/shard_map/pallas_call | solution.py:451
  96.2 1.0 copy.9
  97.2 0.8 copy.10
